TPU v7x, 512 devices: a whole 4x8x8 slice. The times are simulated.
512 devices in a mesh: row: 16 (over y_hi, x), col: 32 (over y_lo, z, core).
Axes of the slice: x: 4, y: 8 (y_hi: 4, y_lo: 2; y = y_hi * 2 + y_lo), z: 8, core: 2. Of those that a mesh axis runs over, the one named last changes fastest.
Arguments:
- queries: bfloat16 [49152, 128], P(('row', 'col')), may hold values from -40 to 40
- keys: bfloat16 [49152, 128], P(('col', 'row')), may hold values from -4 to 4
- values: bfloat16 [49152, 128], P(('col', 'row')), may hold values from -6 to 6
- out_grad: bfloat16 [49152, 128], P(('row', 'col')), may hold values from -6 to 6
- unit_order: int32 [384], replicated, may hold values from 0 to 383, each once
Outputs:
- query_grad: bfloat16 [49152, 128], P(('row', 'col'))
- key_grad: bfloat16 [49152, 128], P(('col', 'row'))
- value_grad: bfloat16 [49152, 128], P(('col', 'row'))
All inputs are finite; a program needn't handle non-finite values.
Results may differ from a plain program's by a relative error of at most 0.0051.
Values may be sent and summed in bfloat16 or wider, within the bound.
A program may use at most 128 MiB of HBM per device.

v0:
```python
import functools
import math

import jax
import jax.numpy as jnp
from jax import lax
from jax.experimental import pallas as pl
from jax.experimental.pallas import tpu as pltpu
from jax.sharding import PartitionSpec as P

UNIT = 128
HD = 128
SHARD = 96
YH, X, YL, Z, CORE = 4, 4, 2, 8, 2
ROWS, COLS = YH * X, YL * Z * CORE
QN, KN = COLS * SHARD, ROWS * SHARD
QUNITS, KUNITS = QN // UNIT, KN // UNIT
QT = YL * CORE * SHARD
KT = X * SHARD
LANE_ROWS = QT // UNIT
MASK_ROWS = 32
SCALE = 1.0 / math.sqrt(HD)
LOG2_SCALE = math.log2(math.e) * SCALE
masked_score = -1e30
lowest_peak = -1e29
least_total = 1e-30

f32 = jnp.float32
bf16 = jnp.bfloat16
MESH = pl.DeviceIdType.MESH
contract_last = (((1,), (1,)), ((), ()))
contract_first = (((0,), (0,)), ((), ()))


def wrap(value, size):
    return lax.rem(value + size, size)


def owner_col(o):
    far = (o + Z // 2) % Z
    return (o % 2) * (Z * CORE) + far * CORE + (o // 2) % 2


def place_queries(units, r, pos_s):
    lane = lax.broadcasted_iota(jnp.int32, (8, QT), 1)
    half = CORE * SHARD
    side = lane // half
    for zz in range(Z):
        token = side * (Z * half) + zz * half + (lane - side * half)
        unit, inside = token // UNIT, token % UNIT
        base = jnp.zeros((8, QT), jnp.int32)
        for a in range(YL):
            first = (a * Z + zz) * half // UNIT
            for u in (first, first + 1):
                base = jnp.where(unit == u, units[r * QUNITS + u], base)
        pos_s[zz] = base * UNIT + inside


def pass_1_tile(units, c, zq, yk, qd, kv, pos_s, p_s, gw_s, peak_s, total_s, dot_s):
    query, grad = qd[0, zq].reshape(QT, HD), qd[1, zq].reshape(QT, HD)
    sub = lax.broadcasted_iota(jnp.int32, (MASK_ROWS // 8, 8, QT), 0) * 8 + lax.broadcasted_iota(
        jnp.int32, (MASK_ROWS // 8, 8, QT), 1
    )
    query_pos = pos_s[zq]
    keys, values = kv[0, yk].reshape(KT, HD), kv[1, yk].reshape(KT, HD)
    all_scores = lax.dot_general(keys, query, contract_last, preferred_element_type=f32)
    all_grads = lax.dot_general(values, grad, contract_last, preferred_element_type=f32)
    for place in range(X):
        rows = slice(place * SHARD, (place + 1) * SHARD)
        scores = all_scores[rows].reshape(SHARD // 8, 8, QT)
        grad_weights = all_grads[rows]
        parts = []
        for b in range(SHARD // MASK_ROWS):
            token = (yk * X + place) * SHARD + b * MASK_ROWS
            key_pos = units[c * KUNITS + token // UNIT] * UNIT + token % UNIT
            part = scores[b * MASK_ROWS // 8:(b + 1) * MASK_ROWS // 8]
            parts.append(
                jnp.where(sub <= (query_pos - key_pos)[None], part * LOG2_SCALE, masked_score)
            )
        scores = jnp.concatenate(parts, axis=0)
        peak = jnp.maximum(jnp.max(scores, axis=0), lowest_peak)
        expos = jnp.exp2(scores - peak[None])
        peak_s[zq, yk, place] = peak
        total_s[zq, yk, place] = jnp.sum(expos, axis=0)
        dot_s[zq, yk, place] = jnp.sum(expos * grad_weights.reshape(SHARD // 8, 8, QT), axis=0)
        p_s[zq, yk, rows, :] = expos.reshape(SHARD, QT)
        gw_s[zq, yk, rows, :] = grad_weights


def row_statistics(zq, peak_s, total_s, dot_s, stat):
    peaks = peak_s[zq].reshape(X * YH, 8, QT)
    peak = jnp.max(jnp.max(peaks, axis=0), axis=0, keepdims=True)
    factors = jnp.exp2(peaks - peak[None])
    total = jnp.sum(total_s[zq].reshape(X * YH, 8, QT) * factors, axis=0)
    dot = jnp.sum(dot_s[zq].reshape(X * YH, 8, QT) * factors, axis=0)
    total = jnp.maximum(jnp.sum(total, axis=0, keepdims=True), least_total)
    dot = jnp.sum(dot, axis=0, keepdims=True)
    lse = peak + jnp.log2(total)
    row_dot = dot / total
    for i in range(LANE_ROWS):
        lanes = slice(i * UNIT, (i + 1) * UNIT)
        stat[zq, i:i + 1, :] = lse[:, lanes]
        stat[zq, LANE_ROWS + i:LANE_ROWS + i + 1, :] = row_dot[:, lanes]


def pass_2_tile(zqs, yks, qd, kv, p_s, gw_s, peak_s, done_stat, dq_acc, dkv_acc, fresh=False):
    weights, grad_scores = [[] for _ in yks], [[] for _ in yks]
    for zq in zqs:
        lse = jnp.concatenate([done_stat[zq, i:i + 1, :] for i in range(LANE_ROWS)], axis=1)
        row_dot = jnp.concatenate(
            [done_stat[zq, LANE_ROWS + i:LANE_ROWS + i + 1, :] for i in range(LANE_ROWS)], axis=1
        )
        for j, yk in enumerate(yks):
            w_parts, g_parts = [], []
            for place in range(X):
                rows = slice(place * SHARD, (place + 1) * SHARD)
                factor = jnp.exp2(peak_s[zq, yk, place] - lse)
                w = p_s[zq, yk, rows, :].reshape(SHARD // 8, 8, QT) * factor[None]
                g = w * (gw_s[zq, yk, rows, :].reshape(SHARD // 8, 8, QT) - row_dot[None])
                w_parts.append(w.reshape(SHARD, QT).astype(bf16))
                g_parts.append(g.reshape(SHARD, QT).astype(bf16))
            weights[j].append(jnp.concatenate(w_parts, axis=0))
            grad_scores[j].append(jnp.concatenate(g_parts, axis=0))
    weights = [jnp.concatenate(row, axis=1) for row in weights]
    grad_scores = [jnp.concatenate(row, axis=1) for row in grad_scores]
    query = jnp.concatenate([qd[0, zq].reshape(QT, HD) for zq in zqs], axis=0)
    grad = jnp.concatenate([qd[1, zq].reshape(QT, HD) for zq in zqs], axis=0)
    for j, yk in enumerate(yks):
        value_part = jnp.dot(weights[j], grad, preferred_element_type=f32)
        key_part = jnp.dot(grad_scores[j], query, preferred_element_type=f32)
        dkv_acc[1, yk] += value_part.reshape(X, SHARD, HD)
        dkv_acc[0, yk] += key_part.reshape(X, SHARD, HD)
    query_part = lax.dot_general(
        jnp.concatenate(grad_scores, axis=0),
        jnp.concatenate([kv[0, yk].reshape(KT, HD) for yk in yks], axis=0),
        contract_first, preferred_element_type=f32,
    )
    for i, zq in enumerate(zqs):
        dq_acc[zq] += query_part[i * QT:(i + 1) * QT].reshape(YL, CORE, SHARD, HD)


def kernel(
    q_ref, k_ref, v_ref, g_ref, units,
    out,
    qd, kv, pos_s, p_s, gw_s, peak_s, total_s, dot_s, stat, inbox, result, done_stat,
    dq_acc, dkv_acc, sib_in, q_sum, zs, zr, ys, yr, xs, xr, kv_sum, hs, hr,
    y_ss, y_rs, z_ss, z_rs, n_ss, n_rs, c_ss, c_rs, h_ss, h_rs, x_ss, x_rs,
    a_ss, a_rs, b_ss, b_rs,
    own_s, rc_ss, rc_rs, rz_ss, rz_rs, ry_ss, ry_rs, rx_ss, rx_rs, rh_ss, rh_rs,
):
    r = lax.axis_index("row")
    c = lax.axis_index("col")
    yh, x = r // X, r % X
    yl, z, co = c // (Z * CORE), (c // CORE) % Z, c % CORE

    def col_of(a, b, d):
        return a * (Z * CORE) + b * CORE + d

    def row_of(a, b):
        return a * X + b

    def at_z(delta):
        return wrap(z + delta, Z)

    def at_x(delta):
        return wrap(x + delta, X)

    def at_y(delta):
        return wrap(yh + delta, YH)

    sibling = (r, col_of(yl, z, 1 - co))
    y_peer = (r, col_of(1 - yl, z, co))
    z_next = [(r, col_of(yl, at_z(1), co)), (r, col_of(yl, at_z(-1), co))]
    x_next = [(row_of(yh, at_x(1)), c), (row_of(yh, at_x(-1)), c), (row_of(yh, at_x(2)), c)]
    way = (1, -1)

    def send(src, dst, send_sem, recv_sem, device):
        copy = pltpu.make_async_remote_copy(
            src_ref=src, dst_ref=dst, send_sem=send_sem, recv_sem=recv_sem,
            device_id=device, device_id_type=MESH,
        )
        copy.start()
        return copy

    def arrive(dst, recv_sem):
        pltpu.make_async_remote_copy(
            src_ref=dst, dst_ref=dst, send_sem=recv_sem, recv_sem=recv_sem,
            device_id=sibling, device_id_type=MESH,
        ).wait_recv()

    barrier = pltpu.get_barrier_semaphore()

    def greet(other, _):
        @pl.when(other != c)
        def _():
            pl.semaphore_signal(barrier, inc=1, device_id=(r, other), device_id_type=MESH)
        return 0

    lax.fori_loop(0, COLS, greet, 0)
    for device in x_next:
        pl.semaphore_signal(barrier, inc=1, device_id=device, device_id_type=MESH)
    for j in range(1, YH):
        pl.semaphore_signal(
            barrier, inc=1, device_id=(row_of(at_y(j), x), c), device_id_type=MESH
        )

    own = [
        pltpu.make_async_copy(src, dst, own_s.at[i])
        for i, (src, dst) in enumerate((
            (q_ref, qd.at[0, z, yl, co]), (g_ref, qd.at[1, z, yl, co]),
            (k_ref, kv.at[0, yh, x]), (v_ref, kv.at[1, yh, x]),
        ))
    ]
    for copy in own:
        copy.start()

    def q_slot(a, b, d):
        return qd.at[:, b, a, d]

    def k_slot(high, xx):
        return kv.at[:, high, xx]

    for copy in own:
        copy.wait()
    pl.semaphore_wait(barrier, COLS - 1 + 3 + YH - 1)

    sent = []

    def core_send(side, zz):
        slot = q_slot(side, zz, co)
        sent.append(send(slot, slot, c_ss.at[side, zz], c_rs.at[side, zz], sibling))

    def x_sends(high, slot):
        for d in range(3):
            sent.append(send(slot, slot, x_ss.at[d, high], x_rs.at[d, high], x_next[d]))

    def z_arrive(*deltas):
        for delta in deltas:
            zz = at_z(delta)
            slot = q_slot(yl, zz, co)
            arrive(slot, z_rs.at[zz])
            if abs(delta) > 1:
                sent.append(send(slot, slot, y_ss.at[zz], y_rs.at[zz], y_peer))
            core_send(yl, zz)

    def y_arrive(*deltas):
        for delta in deltas:
            zz = at_z(delta)
            slot = q_slot(1 - yl, zz, co)
            arrive(slot, y_rs.at[zz])
            if delta == 0:
                for d in range(2):
                    sent.append(send(slot, slot, n_ss.at[d], n_rs.at[d], z_next[d]))
            core_send(1 - yl, zz)

    def near_arrive():
        for d in range(2):
            zz = at_z(-way[d])
            arrive(q_slot(1 - yl, zz, co), n_rs.at[d])
            core_send(1 - yl, zz)

    def h_arrive(j):
        high = at_y(-j)
        slot = k_slot(high, x)
        arrive(slot, h_rs.at[j])
        x_sends(high, slot)

    def x_arrive(delta):
        high = at_y(delta)
        for d in range(3):
            arrive(k_slot(high, at_x((-1, 1, 2)[d])), x_rs.at[d, high])

    def query_ready(zz):
        for side in range(2):
            arrive(q_slot(side, zz, 1 - co), c_rs.at[side, zz])

    def scores_of(count, where):
        def one(i, _):
            dz, dy = where(i)
            pass_1_tile(
                units, c, at_z(dz), at_y(dy), qd, kv, pos_s, p_s, gw_s, peak_s, total_s, dot_s
            )
            return 0

        lax.fori_loop(0, count, one, 0)

    def stat_send(*deltas):
        for delta in deltas:
            row_statistics(at_z(delta), peak_s, total_s, dot_s, stat)
        for delta in deltas:
            zq = at_z(delta)
            target = owner_col(zq)

            @pl.when(target != c)
            def _():
                send(stat.at[zq], inbox.at[c], a_ss.at[zq], a_rs.at[c], (r, target))

            @pl.when(target == c)
            def _():
                inbox[c] = stat[zq]

    mine = q_slot(yl, z, co)
    mine_k = k_slot(yh, x)
    sent.append(send(mine, mine, y_ss.at[z], y_rs.at[z], y_peer))
    for j in (1, 3, 2):
        sent.append(
            send(mine_k, mine_k, h_ss.at[j], h_rs.at[j], (row_of(at_y(j), x), c))
        )
    x_sends(yh, mine_k)
    for delta in (1, -1, 2, -2, 3, -3, 4):
        zz = at_z(delta)
        sent.append(
            send(mine, mine, z_ss.at[zz], z_rs.at[z], (r, col_of(yl, zz, co)))
        )
    core_send(yl, z)
    place_queries(units, r, pos_s)
    result[...] = jnp.zeros_like(result)
    stat[...] = jnp.zeros_like(stat)
    dq_acc[...] = jnp.zeros_like(dq_acc)
    dkv_acc[...] = jnp.zeros_like(dkv_acc)
    y_arrive(0)
    z_arrive(1, -1)
    x_arrive(0)
    query_ready(z)
    scores_of(1, lambda i: (i, 0))
    z_arrive(2, -2)
    h_arrive(1)
    h_arrive(3)
    near_arrive()
    query_ready(at_z(1))
    query_ready(at_z(-1))
    scores_of(2, lambda i: (2 * i - 1, 0))
    h_arrive(2)
    z_arrive(3, -3)
    y_arrive(2, -2)
    query_ready(at_z(2))
    query_ready(at_z(-2))
    scores_of(2, lambda i: (4 * i - 2, 0))
    z_arrive(4)
    x_arrive(-1)
    scores_of(5, lambda i: (i - 2, -1))
    y_arrive(3, -3)
    x_arrive(1)
    scores_of(5, lambda i: (i - 2, 1))
    query_ready(at_z(3))
    query_ready(at_z(-3))
    scores_of(6, lambda i: (6 * (i // 3) - 3, i % 3 - 1))
    y_arrive(4)
    query_ready(at_z(4))
    scores_of(3, lambda i: (4, i - 1))
    x_arrive(2)
    scores_of(4, lambda i: ((2 * (i % 2) - 1) * ((i + 1) // 2), 2))
    stat_send(0, 1, -1, 2)
    scores_of(4, lambda i: ((2 * (i % 2) - 1) * ((i + 5) // 2), 2))
    stat_send(-2, 3, -3, 4)

    def stat_sent(o, _):
        @pl.when(owner_col(o) != c)
        def _():
            pltpu.make_async_remote_copy(
                src_ref=stat.at[o], dst_ref=inbox.at[c], send_sem=a_ss.at[o],
                recv_sem=a_rs.at[c], device_id=(r, owner_col(o)), device_id_type=MESH,
            ).wait_send()
        return 0

    owned = at_z(4)
    partners = [
        (r, col_of(wrap(yl + a, YL), at_z(delta), wrap(co + b, CORE)))
        for delta in (4, 3, -3, 2, -2, 1, -1, 0) for a in (1, 0) for b in (1, 0)
        if (delta, a, b) != (0, 0, 0)
    ]

    def give(partner):
        return pltpu.make_async_remote_copy(
            src_ref=result, dst_ref=done_stat.at[owned], send_sem=b_ss.at[partner[1]],
            recv_sem=b_rs.at[owned], device_id=partner, device_id_type=MESH,
        )

    @pl.when(owner_col(owned) == c)
    def _():
        for partner in reversed(partners):
            arrive(inbox.at[partner[1]], a_rs.at[partner[1]])
        lse = inbox[:, 0:LANE_ROWS, :]
        row_dot = inbox[:, LANE_ROWS:2 * LANE_ROWS, :]
        peak = jnp.max(lse, axis=0)
        part = jnp.exp2(lse - peak[None])
        total = jnp.sum(part, axis=0)
        result[0:LANE_ROWS, :] = peak + jnp.log2(total)
        result[LANE_ROWS:2 * LANE_ROWS, :] = jnp.sum(part * row_dot, axis=0) / total
        for partner in partners:
            give(partner).start()
        done_stat[owned] = result[...]

    def stat_take(zq):
        @pl.when(owner_col(zq) != c)
        def _():
            arrive(done_stat.at[zq], b_rs.at[zq])

    gather_sent = sent
    sent = []

    def grads_of(zqs, yks):
        pass_2_tile(
            [at_z(d) for d in zqs], [at_y(d) for d in yks],
            qd, kv, p_s, gw_s, peak_s, done_stat, dq_acc, dkv_acc,
        )

    def core_start(zz):
        sent.append(
            send(dq_acc.at[zz, :, 1 - co], sib_in.at[zz], rc_ss.at[zz], rc_rs.at[zz], sibling)
        )

    def core_end(zz):
        arrive(sib_in.at[zz], rc_rs.at[zz])
        return (dq_acc[zz, :, co] + sib_in[zz]) * SCALE

    def z_send(zz):
        zs[zz] = core_end(zz).astype(bf16)
        sent.append(
            send(zs.at[zz], zr.at[z], rz_ss.at[zz], rz_rs.at[z], (r, col_of(yl, zz, co)))
        )

    def z_end():
        total = core_end(z)
        for delta in (4, 3, -3, 2, -2, 1, -1):
            zz = at_z(delta)
            arrive(zr.at[zz], rz_rs.at[zz])
            total += zr[zz].astype(f32)
        q_sum[...] = total
        ys[...] = q_sum[1 - yl].astype(bf16)
        sent.append(send(ys, yr, ry_ss, ry_rs, y_peer))

    def y_end():
        arrive(yr, ry_rs)
        out[0] = (q_sum[yl] + yr[...].astype(f32)).astype(bf16)

    def scaled(a):
        return SCALE if a == 0 else 1.0

    def column_send(dy):
        for d in range(3):
            for a in range(2):
                term = dkv_acc[a, at_y(dy), at_x((1, -1, 2)[d])] * scaled(a)
                xs[dy % YH, d, a] = term.astype(bf16)
            sent.append(
                send(xs.at[dy % YH, d], xr.at[dy % YH, d], rx_ss.at[dy % YH, d],
                     rx_rs.at[dy % YH, d], x_next[d])
            )

    def column_end(dy):
        for d in range(3):
            arrive(xr.at[dy % YH, d], rx_rs.at[dy % YH, d])
        for a in range(2):
            total = dkv_acc[a, at_y(dy), x] * scaled(a)
            for d in range(3):
                total += xr[dy % YH, d, a].astype(f32)
            if dy == 0:
                kv_sum[a] = total
            else:
                hs[dy % YH, a] = total.astype(bf16)
        if dy != 0:
            j = dy % YH
            sent.append(
                send(hs.at[j], hr.at[j], rh_ss.at[j], rh_rs.at[j], (row_of(at_y(dy), x), c))
            )

    def high_end():
        for j in range(1, YH):
            arrive(hr.at[j], rh_rs.at[j])
        for a in range(2):
            total = kv_sum[a]
            for j in range(1, YH):
                total += hr[j, a].astype(f32)
            out[1 + a] = total.astype(bf16)

    for pair in ((4, 3), (-3, 2), (-2, 1), (-1, 0)):
        for delta in pair:
            stat_take(at_z(delta))
        grads_of(pair, [2])
    column_send(2)
    grads_of([4], [1, -1])
    grads_of([4], [0])
    core_start(at_z(4))
    grads_of([3, -3], [1, -1])
    z_send(at_z(4))
    grads_of([3, -3], [0])
    core_start(at_z(3))
    core_start(at_z(-3))

    for dy in (1, -1):
        grads_of([2, -2], [dy])
        if dy == 1:
            z_send(at_z(3))
            z_send(at_z(-3))
        grads_of([1, -1], [dy])
        grads_of([0], [dy])
        column_send(dy)
    column_end(2)
    grads_of([2, -2], [0])
    core_start(at_z(2))
    core_start(at_z(-2))
    grads_of([1, -1], [0])
    core_start(at_z(1))
    core_start(at_z(-1))
    z_send(at_z(2))
    z_send(at_z(-2))
    grads_of([0], [0])
    core_start(z)
    column_send(0)
    z_send(at_z(1))
    z_send(at_z(-1))
    column_end(1)
    column_end(-1)
    z_end()
    column_end(0)
    y_end()
    high_end()
    for copy in gather_sent + sent:
        copy.wait_send()
    lax.fori_loop(0, Z, stat_sent, 0)

    @pl.when(owner_col(owned) == c)
    def _():
        for partner in partners:
            give(partner).wait_send()


def parted(whole, *parts):
    for i, part in enumerate(parts):
        part[...] = whole[i]


def shards(queries, keys, values, out_grad, unit_order):
    vmem = pl.BlockSpec(memory_space=pltpu.VMEM)
    dma = pltpu.SemaphoreType.DMA
    shard = jax.ShapeDtypeStruct((SHARD, HD), bf16)
    tile = (SHARD, HD)
    groups = (Z, YH, X, 8, QT)
    whole = pl.pallas_call(
        kernel,
        out_shape=jax.ShapeDtypeStruct((3, SHARD, HD), bf16),
        in_specs=[pl.BlockSpec(memory_space=pl.ANY)] * 4 + [pl.BlockSpec(memory_space=pltpu.SMEM)],
        out_specs=vmem,
        scratch_shapes=[
            pltpu.VMEM((2, Z, YL, CORE) + tile, bf16),
            pltpu.VMEM((2, YH, X) + tile, bf16),
            pltpu.VMEM((Z, 8, QT), jnp.int32),
            pltpu.VMEM((Z, YH, KT, QT), f32),
            pltpu.VMEM((Z, YH, KT, QT), f32),
            pltpu.VMEM(groups, f32),
            pltpu.VMEM(groups, f32),
            pltpu.VMEM(groups, f32),
            pltpu.VMEM((Z, 8, UNIT), f32),
            pltpu.VMEM((COLS, 8, UNIT), f32),
            pltpu.VMEM((8, UNIT), f32),
            pltpu.VMEM((Z, 8, UNIT), f32),
            pltpu.VMEM((Z, YL, CORE) + tile, f32),
            pltpu.VMEM((2, YH, X) + tile, f32),
            pltpu.VMEM((Z, YL) + tile, f32),
            pltpu.VMEM((YL,) + tile, f32),
            pltpu.VMEM((Z, YL) + tile, bf16),
            pltpu.VMEM((Z, YL) + tile, bf16),
            pltpu.VMEM(tile, bf16),
            pltpu.VMEM(tile, bf16),
            pltpu.VMEM((YH, 3, 2) + tile, bf16),
            pltpu.VMEM((YH, 3, 2) + tile, bf16),
            pltpu.VMEM((2,) + tile, f32),
            pltpu.VMEM((YH, 2) + tile, bf16),
            pltpu.VMEM((YH, 2) + tile, bf16),
            dma((Z,)), dma((Z,)),
            dma((Z,)), dma((Z,)),
            dma((2,)), dma((2,)),
            dma((YL, Z)), dma((YL, Z)),
            dma((YH,)), dma((YH,)),
            dma((3, YH)), dma((3, YH)),
            dma((Z,)), dma((COLS,)),
            dma((COLS,)), dma((Z,)),
            dma((4,)),
            dma((Z,)), dma((Z,)),
            dma((Z,)), dma((Z,)),
            dma, dma,
            dma((YH, 3)), dma((YH, 3)),
            dma((YH,)), dma((YH,)),
        ],
        compiler_params=pltpu.CompilerParams(
            collective_id=0, has_side_effects=True, vmem_limit_bytes=60 * 2**20
        ),
    )(queries, keys, values, out_grad, unit_order)
    return pl.pallas_call(
        parted,
        out_shape=(shard, shard, shard),
        in_specs=[vmem],
        out_specs=(vmem, vmem, vmem),
    )(whole)


def solution(mesh):
    placed = (
        P(("row", "col"), None),
        P(("col", "row"), None),
        P(("col", "row"), None),
        P(("row", "col"), None),
        P(),
    )
    return jax.shard_map(
        shards,
        mesh=mesh,
        in_specs=placed,
        out_specs=(P(("row", "col"), None), P(("col", "row"), None), P(("col", "row"), None)),
        check_vma=False,
    )
```

profile of v0, /device:TPU:1, one launch (start us, length us, event | category | flops | bytes accessed | tf_op | source)
XLA Modules:
  0.0 74.2 jit_solution(5377485992555569323)
XLA Ops:
  0.6 72.0 %shard_map.76.whole = bf16[3,96,128]{2,1,0:T(8,128)(2,1)} custom-call(bf16[96,128]{1,0:T(8,128)(2,1)} %q_ref.1, bf16[96,128]{1,0:T(8,128)(2,1)} %k_ref.1, bf16[96,128]{1,0:T(8,128)(2,1)} %v_ref.1, bf16[96,128]{1,0:T(8,128)(2,1)} %g_ref.1, s32[384]{0:T(512)} %units.1), custom_call_target="tpu_custom_call" | custom-call | tf_op jit(solution)/shard_map/pallas_call | solution.py:539
  72.7 1.5 %shard_map.77 = (bf16[96,128]{1,0:T(8,128)(2,1)}, bf16[96,128]{1,0:T(8,128)(2,1)}, bf16[96,128]{1,0:T(8,128)(2,1)}) custom-call(bf16[3,96,128]{2,1,0:T(8,128)(2,1)} %shard_map.76.whole), custom_call_target="tpu_custom_call" | custom-call | tf_op jit(solution)/shard_map/pallas_call | solution.py:589
where the time goes:
time: 74.4 us; the launch traced here: 74.2 us
  Pallas kernels  73.5 us (99%)
    pallas_call x1, Pallas kernels, shards(): pl.pallas_call(kernel, out_shape=jax.ShapeDtypeStruct((3, SHARD, HD), bf1...  72 us
    pallas_call x1, Pallas kernels, shards(): pl.pallas_call(parted, out_shape=(shard, shard, shard), in_specs=[vmem],...  1.51 us

commit v1 on v0

--- a/solution.py
+++ b/solution.py
@@ -190,13 +190,13 @@
 
     barrier = pltpu.get_barrier_semaphore()
 
-    def greet(other, _):
-        @pl.when(other != c)
-        def _():
-            pl.semaphore_signal(barrier, inc=1, device_id=(r, other), device_id_type=MESH)
-        return 0
-
-    lax.fori_loop(0, COLS, greet, 0)
+    partners = [
+        (r, col_of(wrap(yl + a, YL), at_z(delta), wrap(co + b, CORE)))
+        for delta in (4, 3, -3, 2, -2, 1, -1, 0) for a in (1, 0) for b in (1, 0)
+        if (delta, a, b) != (0, 0, 0)
+    ]
+    for device in partners:
+        pl.semaphore_signal(barrier, inc=1, device_id=device, device_id_type=MESH)
     for device in x_next:
         pl.semaphore_signal(barrier, inc=1, device_id=device, device_id_type=MESH)
     for j in range(1, YH):
@@ -282,7 +282,7 @@
             )
             return 0
 
-        lax.fori_loop(0, count, one, 0)
+        lax.fori_loop(0, count, one, 0, unroll=count)
 
     def stat_send(*deltas):
         for delta in deltas:
@@ -364,11 +364,6 @@
         return 0
 
     owned = at_z(4)
-    partners = [
-        (r, col_of(wrap(yl + a, YL), at_z(delta), wrap(co + b, CORE)))
-        for delta in (4, 3, -3, 2, -2, 1, -1, 0) for a in (1, 0) for b in (1, 0)
-        if (delta, a, b) != (0, 0, 0)
-    ]
 
     def give(partner):
         return pltpu.make_async_remote_copy(

time: 74.4 us -> 71.7 us (0.964)
  Pallas kernels: 73.5 us -> 70.8 us
    pallas_call x1, Pallas kernels: 72 us -> 69.3 us  [shards(): pl.pallas_call(kernel, out_shape=jax.ShapeDtypeStruct((3, SHARD, HD), bf1...]
where the time goes in v1:
time: 71.7 us; the launch traced here: 71.5 us
  Pallas kernels  70.8 us (99%)
    pallas_call x1, Pallas kernels, shards(): pl.pallas_call(kernel, out_shape=jax.ShapeDtypeStruct((3, SHARD, HD), bf1...  69.3 us
    pallas_call x1, Pallas kernels, shards(): pl.pallas_call(parted, out_shape=(shard, shard, shard), in_specs=[vmem],...  1.51 us

profile of v1, /device:TPU:1, one launch (start us, length us, event | category | flops | bytes accessed | tf_op | source)
XLA Modules:
  0.0 71.5 jit_solution(8329443022887787312)
XLA Ops:
  0.6 69.3 %shard_map.76.whole = bf16[3,96,128]{2,1,0:T(8,128)(2,1)} custom-call(bf16[96,128]{1,0:T(8,128)(2,1)} %q_ref.1, bf16[96,128]{1,0:T(8,128)(2,1)} %k_ref.1, bf16[96,128]{1,0:T(8,128)(2,1)} %v_ref.1, bf16[96,128]{1,0:T(8,128)(2,1)} %g_ref.1, s32[384]{0:T(512)} %units.1), custom_call_target="tpu_custom_call" | custom-call | tf_op jit(solution)/shard_map/pallas_call | solution.py:534
  70.0 1.5 %shard_map.77 = (bf16[96,128]{1,0:T(8,128)(2,1)}, bf16[96,128]{1,0:T(8,128)(2,1)}, bf16[96,128]{1,0:T(8,128)(2,1)}) custom-call(bf16[3,96,128]{2,1,0:T(8,128)(2,1)} %shard_map.76.whole), custom_call_target="tpu_custom_call" | custom-call | tf_op jit(solution)/shard_map/pallas_call | solution.py:584

commit v2 on v1

--- a/solution.py
+++ b/solution.py
@@ -483,13 +483,11 @@
     core_start(at_z(-3))
 
     for dy in (1, -1):
-        grads_of([2, -2], [dy])
+        grads_of([2, -2, 1, -1, 0], [dy])
+        column_send(dy)
         if dy == 1:
             z_send(at_z(3))
             z_send(at_z(-3))
-        grads_of([1, -1], [dy])
-        grads_of([0], [dy])
-        column_send(dy)
     column_end(2)
     grads_of([2, -2], [0])
     core_start(at_z(2))

time: 71.7 us -> 71 us (level)
  no operation moved by 1% of the time
where the time goes in v2:
time: 71 us; the launch traced here: 70.8 us
  Pallas kernels  70.1 us (99%)
    pallas_call x1, Pallas kernels, shards(): pl.pallas_call(kernel, out_shape=jax.ShapeDtypeStruct((3, SHARD, HD), bf1...  68.6 us
    pallas_call x1, Pallas kernels, shards(): pl.pallas_call(parted, out_shape=(shard, shard, shard), in_specs=[vmem],...  1.51 us

profile of v2, /device:TPU:1, one launch (start us, length us, event | category | flops | bytes accessed | tf_op | source)
XLA Modules:
  0.0 70.8 jit_solution(17855689084129479231)
XLA Ops:
  0.6 68.6 %shard_map.76.whole = bf16[3,96,128]{2,1,0:T(8,128)(2,1)} custom-call(bf16[96,128]{1,0:T(8,128)(2,1)} %q_ref.1, bf16[96,128]{1,0:T(8,128)(2,1)} %k_ref.1, bf16[96,128]{1,0:T(8,128)(2,1)} %v_ref.1, bf16[96,128]{1,0:T(8,128)(2,1)} %g_ref.1, s32[384]{0:T(512)} %units.1), custom_call_target="tpu_custom_call" | custom-call | tf_op jit(solution)/shard_map/pallas_call | solution.py:532
  69.3 1.5 %shard_map.77 = (bf16[96,128]{1,0:T(8,128)(2,1)}, bf16[96,128]{1,0:T(8,128)(2,1)}, bf16[96,128]{1,0:T(8,128)(2,1)}) custom-call(bf16[3,96,128]{2,1,0:T(8,128)(2,1)} %shard_map.76.whole), custom_call_target="tpu_custom_call" | custom-call | tf_op jit(solution)/shard_map/pallas_call | solution.py:582
